TPU v7x, 128 devices: a whole 4x4x4 slice. The times are simulated.
128 devices in a mesh: seq: 16 (over y, x), mp: 8 (over z, core).
Axes of the slice: x: 4, y: 4, z: 4, core: 2. Of those that a mesh axis runs over, the one named last changes fastest.
Arguments:
- residual_activations: bfloat16 [16384, 4096], P('seq', 'mp'), may hold values from -6 to 6
- prelayer_gain_vector: bfloat16 [4096], replicated, may hold values from 0.099609375 to 1.8984375
- gating_projection: bfloat16 [4096], replicated, may hold values from -0.25 to 0.25
- asker_projection: bfloat16 [4096, 8192], P(None, 'mp'), may hold values from -0.09375 to 0.09375
- lookup_projection: bfloat16 [4096, 1024], P(None, 'mp'), may hold values from -0.09375 to 0.09375
- content_projection: bfloat16 [4096, 1024], P(None, 'mp'), may hold values from -0.09375 to 0.09375
- final_projection: bfloat16 [8192, 4096], P(None, 'mp'), may hold values from -0.0625 to 0.0625
- logit_sharpness: float32 [64], P('mp'), may hold values from 1 to 64
- selection_table: int32 [16, 256], P('seq'), may hold values from 0 to 1023, as said below
- dispatched_tally_table: int32 [16, 16], replicated, may hold values from 0 to 16, as said below
Outputs:
- blended: bfloat16 [16384, 4096], P('seq', 'mp')
Inputs may be any that keep to these rules, and one draw needn't show every extreme that they name: `dispatched_tally_table`: entry [s, d] counts the routed tokens of source shard s whose compacted place falls to owner d: the compacted sequence lists all routed tokens in sequence order and is dealt in blocks of 8 places, block b to owner b mod 16. Every entry is a multiple of 8, and every column sums to 128. `selection_table`: row s lists in increasing order the distinct local indices of the routed tokens of source shard s, as many as row s of dispatched_tally_table sums to, and zeros after them.
All inputs are finite; a program needn't handle non-finite values.
Results may differ from a plain program's by a relative error of at most 0.0059.
Values may be sent and summed in bfloat16 or wider, within the bound.
No kernel may reach another device: no remote copies, remote signals or barrier semaphores. Data moves between devices by JAX's collectives and lax.ppermute only.
A program may use at most 64 MiB of HBM per device.

v0:
```python
import math
import jax
import jax.numpy as jnp
from jax import lax
from jax.sharding import PartitionSpec as P

HEADS = 64
SHARED_KV_COUNT = 8
PER_HEAD_DIM = 128
SEL = 128


def compact(incoming, prefix, spans, shard, nseq, owned):
    span_ids = jnp.arange(nseq, dtype=jnp.int32) * nseq + shard
    source_of = jnp.sum(
        (prefix[None, :] + spans[None, :] <= span_ids[:, None]).astype(jnp.int32), axis=1
    )
    matches = source_of[:, None] == jnp.arange(nseq, dtype=jnp.int32)[None, :]
    start_of = jnp.sum(jnp.where(matches, prefix[None, :], 0), axis=1)
    half_of = (span_ids - start_of) // nseq
    blocks = incoming.reshape(2 * nseq, incoming.shape[2], incoming.shape[3])
    return blocks[half_of * nseq + source_of].reshape(owned, incoming.shape[3])


def build_return(delta, prefix, spans, shard, nseq, block_rows):
    first = (shard - prefix) % nseq
    counter = jnp.arange(2, dtype=jnp.int32)[:, None] * nseq + first[None, :]
    usable = counter < spans[None, :]
    target = jnp.minimum((prefix[None, :] + counter) // nseq, nseq - 1)
    blocks = delta.reshape(nseq, block_rows, delta.shape[1])[target]
    return jnp.where(usable[:, :, None, None], blocks, jnp.zeros_like(blocks))


def on_device(
    residual_activations,
    prelayer_gain_vector,
    gating_projection,
    asker_projection,
    lookup_projection,
    content_projection,
    final_projection,
    logit_sharpness,
    selection_table,
    dispatched_tally_table,
):
    nseq = lax.axis_size("seq")
    shard = lax.axis_index("seq")
    owned = SEL
    block_rows = owned // nseq
    slots = selection_table.shape[1]
    sent = jnp.sum(dispatched_tally_table, axis=1)
    spans = sent // block_rows
    prefix = jnp.cumsum(spans) - spans
    mine = jnp.arange(nseq, dtype=jnp.int32) == shard
    my_prefix = jnp.sum(jnp.where(mine, prefix, 0))
    my_sent = jnp.sum(jnp.where(mine, sent, 0))
    rotation = my_prefix % nseq
    index_list = selection_table[0]
    live = jnp.arange(slots) < my_sent
    gathered_rows = residual_activations[index_list]
    gathered_rows = jnp.where(live[:, None], gathered_rows, jnp.zeros_like(gathered_rows))
    whole_rows = lax.all_gather(gathered_rows, "mp", axis=1, tiled=True)
    outgoing = jnp.roll(
        whole_rows.reshape(2, nseq, block_rows, whole_rows.shape[1]), rotation, axis=1
    )
    incoming = lax.all_to_all(outgoing, "seq", split_axis=1, concat_axis=1, tiled=True)
    full = compact(incoming, prefix, spans, shard, nseq, owned)
    gate = jax.nn.sigmoid(jnp.dot(full, gating_projection, preferred_element_type=jnp.float32))
    widened = full.astype(jnp.float32)
    inverse = lax.rsqrt(jnp.mean(widened * widened, axis=1, keepdims=True) + 1e-05)
    normed = (widened * inverse * prelayer_gain_vector.astype(jnp.float32)).astype(jnp.bfloat16)
    query = jnp.dot(normed, asker_projection, preferred_element_type=jnp.float32).astype(
        jnp.bfloat16
    )
    keys = jnp.dot(normed, lookup_projection, preferred_element_type=jnp.float32).astype(
        jnp.bfloat16
    )
    values = jnp.dot(normed, content_projection, preferred_element_type=jnp.float32).astype(
        jnp.bfloat16
    )
    paired = jnp.stack([keys, values])
    memory_pair_portion = lookup_projection.shape[1] // PER_HEAD_DIM
    asker_cluster = HEADS // SHARED_KV_COUNT
    query_heads = query.reshape(owned, memory_pair_portion, asker_cluster, PER_HEAD_DIM)
    gating_multipliers = logit_sharpness.reshape(memory_pair_portion, asker_cluster) / math.sqrt(
        PER_HEAD_DIM
    )
    own_slots = jnp.arange(owned, dtype=jnp.int32)
    query_places = (
        own_slots // block_rows * nseq * block_rows + shard * block_rows + own_slots % block_rows
    )
    start_best = jnp.full((memory_pair_portion, asker_cluster, owned), -1e30, jnp.float32)
    piece = lax.all_gather(paired, "seq", axis=1, tiled=True)
    best = start_best
    count = piece.shape[1]
    key_piece = piece[0].reshape(count, memory_pair_portion, PER_HEAD_DIM)
    value_piece = piece[1].reshape(count, memory_pair_portion, PER_HEAD_DIM)
    index_all = jnp.arange(count, dtype=jnp.int32)
    owner = index_all // owned
    position = index_all % owned
    key_places = (
        position // block_rows * nseq * block_rows + owner * block_rows + position % block_rows
    )
    allowed = key_places[None, :] <= query_places[:, None]
    score = jnp.einsum("qngd,knd->ngqk", query_heads, key_piece, preferred_element_type=jnp.float32)
    score = jnp.where(allowed[None, None], score * gating_multipliers[:, :, None, None], -1e30)
    new_best = jnp.maximum(best, jnp.max(score, axis=3))
    weights = jnp.where(allowed[None, None], jnp.exp(score - new_best[..., None]), 0.0)
    totals = jnp.sum(weights, axis=3)
    mixed = jnp.einsum(
        "ngqk,knd->ngqd",
        weights.astype(jnp.bfloat16),
        value_piece,
        preferred_element_type=jnp.float32,
    )
    sums = mixed
    best, totals, sums = (new_best, totals, sums)
    attended = (sums / totals[..., None]).astype(jnp.bfloat16)
    attended = attended.transpose(2, 0, 1, 3).reshape(
        owned, memory_pair_portion * asker_cluster * PER_HEAD_DIM
    )
    projected = jnp.dot(
        lax.all_gather(attended, "mp", axis=1, tiled=True),
        final_projection,
        preferred_element_type=jnp.float32,
    )
    delta = (gate[:, None] * projected).astype(jnp.bfloat16)
    outgoing_back = build_return(delta, prefix, spans, shard, nseq, block_rows)
    coming_back = lax.all_to_all(outgoing_back, "seq", split_axis=1, concat_axis=1, tiled=True)
    restored = jnp.roll(coming_back, -rotation, axis=1).reshape(slots, delta.shape[1])
    restored = jnp.where(live[:, None], restored, jnp.zeros_like(restored))
    updated = (
        residual_activations.astype(jnp.float32).at[index_list].add(restored.astype(jnp.float32))
    )
    return updated.astype(jnp.bfloat16)


def solution(mesh):
    placed = (
        P("seq", "mp"),
        P(),
        P(),
        P(None, "mp"),
        P(None, "mp"),
        P(None, "mp"),
        P(None, "mp"),
        P("mp"),
        P("seq", None),
        P(),
    )
    return jax.shard_map(
        on_device, mesh=mesh, in_specs=placed, out_specs=P("seq", "mp"), check_vma=False
    )
```

profile of v0, /device:TPU:1, one launch (start us, length us, event | category | flops | bytes accessed | tf_op | source)
XLA Modules:
  0.0 201.7 jit_solution(617594323271170253)
XLA Ops:
  6.5 0.9 reduce_sum.69
  7.5 0.1 copy.35
  7.6 0.1 reduce.3
  7.7 0.6 and_select_fusion.4
  8.3 0.6 iota_compare_fusion.1
  9.0 0.7 compare_select_fusion
  9.7 2.6 %gather_fusion = bf16[256,512]{1,0:T(8,128)(2,1)S(1)} fusion(bf16[1024,512]{1,0:T(8,128)(2,1)} %param.10, s32[1024]{0:T(1024)S(1)} %pad_clamp_fusion.2), kind=kCustom, calls=%fused_computation | custom fusion | bytes 525312 | tf_op jit(solution)/shard_map/gather | solution.py:60
  12.3 0.8 broadcast_select_fusion
  13.1 0.0 all-gather.4.cloned.1.call-update
  13.1 0.6 fusion.52
  15.6 26.6 %all-gather.4.cloned.1.call-done = bf16[256,4096]{1,0:T(8,128)(2,1)} async-done(((bf16[256,512]{1,0:T(8,128)(2,1)}), bf16[256,4096]{1,0:T(8,128)(2,1)}) %all-gather.4.cloned.1.call-update) | async-done | bytes 2097168 | tf_op jit(solution)/shard_map/all_gather | solution.py:62
  42.3 2.4 %fusion.7 = bf16[2,16,8,4096]{3,2,1,0:T(8,128)(2,1)S(1)} fusion(s32[]{:T(128)S(6)} %select_n.208, bf16[2,16,8,4096]{3,2,1,0:T(8,128)(2,1)} %bitcast.124), kind=kLoop, calls=%fused_computation.15 | loop fusion | flops 1048576 | bytes 4194308 | tf_op jit(solution)/shard_map/jit(_roll_dynamic)/concatenate | solution.py:63
  44.6 1.5 copy.48
  46.1 6.6 %all-to-all-start = ((bf16[2,16,8,4096]{3,2,0,1:T(8,128)(2,1)}), bf16[2,16,8,4096]{3,2,0,1:T(8,128)(2,1)S(1)}, u32[]{:S(2)}, u32[]{:S(2)}) async-start(bf16[2,16,8,4096]{3,2,0,1:T(8,128)(2,1)} %copy.48), calls=%async_computation | async-start | bytes 4194304 | tf_op jit(solution)/shard_map/all_to_all | solution.py:66
  52.8 0.0 all-gather.6.cloned.1.call-start
  52.8 0.2 convert_reduce_fusion
  53.0 0.2 select_reduce_fusion
  53.2 32.2 %all-to-all-done = bf16[2,16,8,4096]{3,2,0,1:T(8,128)(2,1)S(1)} async-done(((bf16[2,16,8,4096]{3,2,0,1:T(8,128)(2,1)}), bf16[2,16,8,4096]{3,2,0,1:T(8,128)(2,1)S(1)}, u32[]{:S(2)}, u32[]{:S(2)}) %all-to-all-start) | async-done | bytes 2097184 | tf_op jit(solution)/shard_map/all_to_all | solution.py:66
  85.4 1.5 copy.38
  86.9 2.2 %gather_fusion.1 = bf16[16,8,4096]{2,1,0:T(8,128)(2,1)S(1)} fusion(bf16[32,8,4096]{2,1,0:T(8,128)(2,1)} %bitcast.123, s32[1024]{0:T(1024)S(1)} %pad_clamp_fusion.1), kind=kCustom, calls=%fused_computation.1 | custom fusion | bytes 2097216 | tf_op jit(solution)/shard_map/gather | solution.py:22
  89.1 0.3 multiply_reduce_fusion
  89.4 0.1 rsqrt.12
  89.5 0.5 fusion.11
  90.0 1.7 fusion.12
  91.8 0.6 pad_maximum_fusion
  92.4 0.0 all-gather.8.cloned.1.call-start
  92.5 0.3 broadcast_compare_fusion
  92.9 4.7 %fusion.8 = bf16[16,8,8,128]{3,2,1,0:T(8,128)(2,1)S(1)} fusion(bf16[4096,1024]{1,0:T(8,128)(2,1)} %param.13, bf16[16,8,4096]{2,1,0:T(8,128)(2,1)S(1)} %gather_fusion.1, f32[4096]{0:T(1024)S(1)} %convert_element_type.49, f32[128]{0:T(128)S(1)} %rsqrt.12), kind=kOutput, calls=%fused_computation.20 | convolution fusion | flops 1075970048 | bytes 9716224 | tf_op jit(solution)/shard_map/dot_general | solution.py:72
  97.6 34.0 %all-gather.6.cloned.1.call-done = bf16[2,2048,128]{2,1,0:T(8,128)(2,1)} async-done(((bf16[2,128,128]{2,1,0:T(8,128)(2,1)}), bf16[2,2048,128]{2,1,0:T(8,128)(2,1)}) %all-gather.6.cloned.1.call-update) | async-done | bytes 1048592 | tf_op jit(solution)/shard_map/all_gather | solution.py:93
  131.6 2.3 %fusion = (f32[8,128]{1,0:T(8,128)S(1)}, f32[2048,128,8]{1,0,2:T(8,128)S(1)}) fusion(f32[8]{0:T(128)S(1)} %broadcast_multiply_fusion, pred[128,2048]{0,1:T(8,128)(4,1)S(1)} %broadcast_compare_fusion, bf16[16,8,8,128]{3,2,1,0:T(8,128)(2,1)S(1)} %fusion.8, bf16[2,2048,128]{2,1,0:T(8,128)(2,1)} %all-gather.6.cloned.1.call-done), kind=kOutput, calls=%fused_computation.7 | convolution fusion | flops 543161344 | bytes 9441312 | tf_op jit(solution)/shard_map/qngd,knd->ngqk/dot_general | solution.py:105
  133.9 2.1 %fusion.1 = f32[8,128]{1,0:T(8,128)S(1)} fusion(f32[2048,128,8]{1,0,2:T(8,128)S(1)} %get-tuple-element.10, f32[8,128]{1,0:T(8,128)S(1)} %broadcast_maximum_fusion, f32[8]{0:T(128)S(1)} %broadcast_multiply_fusion, pred[128,2048]{0,1:T(8,128)(4,1)S(1)} %broadcast_compare_fusion), kind=kLoop, calls=%fused_computation.8 | loop fusion | flops 10484736 | bytes 8658976 | tf_op jit(solution)/shard_map/reduce_sum | solution.py:109
  136.0 2.8 %fusion.21 = bf16[8,128,128]{1,2,0:T(8,128)(2,1)} fusion(f32[2048,128,8]{1,0,2:T(8,128)S(1)} %get-tuple-element.10, f32[8,128]{1,0:T(8,128)S(1)} %broadcast_maximum_fusion, f32[8]{0:T(128)S(1)} %broadcast_multiply_fusion, pred[128,2048]{0,1:T(8,128)(4,1)S(1)} %broadcast_compare_fusion, bf16[2,2048,128]{2,1,0:T(8,128)(2,1)S(1)} %copy-done.2, ...), kind=kOutput, calls=%fused_computation.34 | convolution fusion | flops 547618816 | bytes 9445888 | tf_op jit(solution)/shard_map/ngqk,knd->ngqd/dot_general | solution.py:110
  138.9 0.1 compare_select_fusion.1
  139.0 0.1 reshape.597
  139.1 0.1 add_compare_fusion
  139.2 0.4 fusion.16
  139.5 26.0 %all-gather.8.cloned.1.call-done = bf16[128,8192]{0,1:T(8,128)(2,1)} async-done(((bf16[128,1024]{0,1:T(8,128)(2,1)}), bf16[128,8192]{0,1:T(8,128)(2,1)}) %all-gather.8.cloned.1.call-update) | async-done | bytes 2097168 | tf_op jit(solution)/shard_map/all_gather | solution.py:123
  165.5 5.3 %fusion.10 = bf16[16,8,512]{2,1,0:T(8,128)(2,1)S(1)} fusion(bf16[128,8192]{0,1:T(8,128)(2,1)} %all-gather.8.cloned.1.call-done, bf16[8192,512]{1,0:T(8,128)(2,1)} %param.16, f32[128]{0:T(128)S(1)} %fusion.16), kind=kOutput, calls=%fused_computation.22 | convolution fusion | flops 1073872896 | bytes 10617344 | tf_op jit(solution)/shard_map/dot_general | solution.py:122
  170.9 0.6 gather_fusion.2
  171.4 0.1 broadcast_select_fusion.1
  171.5 0.7 copy.42
  172.3 6.5 %all-to-all-start.1 = ((bf16[2,16,8,512]{3,2,0,1:T(8,128)(2,1)}), bf16[2,16,8,512]{3,2,0,1:T(8,128)(2,1)S(1)}, u32[]{:S(2)}, u32[]{:S(2)}) async-start(bf16[2,16,8,512]{3,2,0,1:T(8,128)(2,1)} %copy.42), calls=%async_computation.1 | async-start | bytes 524288 | tf_op jit(solution)/shard_map/all_to_all | solution.py:129
  178.8 1.6 convert_element_type.45
  180.5 6.6 %all-to-all-done.1 = bf16[2,16,8,512]{3,2,0,1:T(8,128)(2,1)S(1)} async-done(((bf16[2,16,8,512]{3,2,0,1:T(8,128)(2,1)}), bf16[2,16,8,512]{3,2,0,1:T(8,128)(2,1)S(1)}, u32[]{:S(2)}, u32[]{:S(2)}) %all-to-all-start.1) | async-done | bytes 262176 | tf_op jit(solution)/shard_map/all_to_all | solution.py:129
  187.0 0.1 fusion.27
  187.2 0.1 bitcast_select_fusion.1
  187.3 5.2 %scatter_custom_fusion = f32[1024,512]{1,0:T(8,128)} fusion(f32[1024,512]{1,0:T(8,128)} %convert_element_type.45, s32[256]{0:T(256)S(1)} %bitcast.128, bf16[256,512]{1,0:T(8,128)(2,1)S(1)} %bitcast_select_fusion.1), kind=kCustom, calls=%fused_computation.40 | custom fusion | flops 262144 | bytes 2359296 | tf_op jit(solution)/shard_map/scatter-add | solution.py:133
  192.5 2.7 %convert_element_type.59 = bf16[1024,512]{1,0:T(8,128)(2,1)} convert(f32[1024,512]{1,0:T(8,128)} %scatter_custom_fusion) | non-fusion elementwise | flops 524288 | bytes 3145728 | tf_op jit(solution)/shard_map/convert_element_type | solution.py:135
  (30 shorter events, 0.2 us)
Async XLA Ops:
  6.5 82.9 %copy-start = (bf16[4096,128]{1,0:T(8,128)(2,1)S(1)}, bf16[4096,128]{1,0:T(8,128)(2,1)}, u32[]{:S(2)}) copy-start(bf16[4096,128]{1,0:T(8,128)(2,1)} %param.14) | copy-start | bytes 3145732
  6.5 35.7 %all-gather.4.cloned.1.call-start = ((), (), s32[]{:S(2)}) async-start(), calls=%async_computation.2 | async-start | bytes 2359296 | tf_op jit(solution)/shard_map/all_gather | solution.py:62
  46.1 6.7 %copy-start.3 = (bf16[4096]{0:T(1024)(128)(2,1)S(1)}, bf16[4096]{0:T(1024)(128)(2,1)}, u32[]{:S(2)}) copy-start(bf16[4096]{0:T(1024)(128)(2,1)} %param.11) | copy-start | bytes 24580
  46.1 39.3 %all-to-all-start = ((bf16[2,16,8,4096]{3,2,0,1:T(8,128)(2,1)}), bf16[2,16,8,4096]{3,2,0,1:T(8,128)(2,1)S(1)}, u32[]{:S(2)}, u32[]{:S(2)}) async-start(bf16[2,16,8,4096]{3,2,0,1:T(8,128)(2,1)} %copy.48), calls=%async_computation | async-start | bytes 4194304 | tf_op jit(solution)/shard_map/all_to_all | solution.py:66
  52.8 78.8 %all-gather.6.cloned.1.call-start = ((), (), s32[]{:S(2)}) async-start(), calls=%async_computation.3 | async-start | bytes 1114112 | tf_op jit(solution)/shard_map/all_gather | solution.py:93
  90.0 2.5 %copy-start.5 = (f32[8]{0:T(128)S(1)}, f32[8]{0:T(128)}, u32[]{:S(2)}) copy-start(f32[8]{0:T(128)} %param.17) | copy-start | bytes 100
  92.4 73.1 %all-gather.8.cloned.1.call-start = ((), (), s32[]{:S(2)}) async-start(), calls=%async_computation.4 | async-start | bytes 2359296 | tf_op jit(solution)/shard_map/all_gather | solution.py:123
  133.9 2.1 %copy-start.2 = (bf16[2,2048,128]{2,1,0:T(8,128)(2,1)S(1)}, bf16[2,2048,128]{2,1,0:T(8,128)(2,1)}, u32[]{:S(2)}) copy-start(bf16[2,2048,128]{2,1,0:T(8,128)(2,1)} %all-gather.6.cloned.1.call-done) | copy-start | bytes 3145732
  136.0 2.8 %copy-start.4 = (bf16[4096]{0:T(1024)(128)(2,1)S(1)}, bf16[4096]{0:T(1024)(128)(2,1)}, u32[]{:S(2)}) copy-start(bf16[4096]{0:T(1024)(128)(2,1)} %param.12) | copy-start | bytes 24580
  170.8 8.0 %copy-start.1 = (bf16[1024,512]{1,0:T(8,128)(2,1)S(1)}, bf16[1024,512]{1,0:T(8,128)(2,1)}, u32[]{:S(2)}) copy-start(bf16[1024,512]{1,0:T(8,128)(2,1)} %param.10) | copy-start | bytes 3145732
  172.3 14.8 %all-to-all-start.1 = ((bf16[2,16,8,512]{3,2,0,1:T(8,128)(2,1)}), bf16[2,16,8,512]{3,2,0,1:T(8,128)(2,1)S(1)}, u32[]{:S(2)}, u32[]{:S(2)}) async-start(bf16[2,16,8,512]{3,2,0,1:T(8,128)(2,1)} %copy.42), calls=%async_computation.1 | async-start | bytes 524288 | tf_op jit(solution)/shard_map/all_to_all | solution.py:129
Sparse Core Ops, SparseCore 0:
  13.2 29.0 all-gather.3
  92.5 38.9 all-gather.5
  139.0 26.4 all-gather.7
where the time goes:
time: 202 us
  waiting for transfers between devices  125 us (62%)
  other arithmetic  20.7 us (10%)
  matrix products  17.7 us (9%)
  between operations  15.3 us (8%)
  starting transfers between devices  13.2 us (7%)
  local copies, waits for them, and re-layouts  9.37 us (5%)
    all_gather x1, waiting for transfers between devices, on_device(): piece = lax.all_gather(paired, 'seq', axis=1, tiled=True)  34 us
    all_to_all x1, waiting for transfers between devices, on_device(): lax.all_to_all(outgoing, 'seq', split_axis=1, concat_axis=1, tiled=True)  32.2 us
    all_gather x1, waiting for transfers between devices, on_device(): whole_rows = lax.all_gather(gathered_rows, 'mp', axis=1, tiled=True)  26.6 us
    all_gather x1, waiting for transfers between devices, on_device(): lax.all_gather(attended, 'mp', axis=1, tiled=True)  26 us
    all_to_all x1, starting transfers between devices, on_device(): lax.all_to_all(outgoing, 'seq', split_axis=1, concat_axis=1, tiled=True)  6.64 us
    all_to_all x1, waiting for transfers between devices, on_device(): lax.all_to_all(outgoing_back, 'seq', split_axis=1, concat_axis=1, tiled=T...  6.56 us
    all_to_all x1, starting transfers between devices, on_device(): lax.all_to_all(outgoing_back, 'seq', split_axis=1, concat_axis=1, tiled=T...  6.52 us
    dot_general x1, matrix products, on_device(): jnp.dot(lax.all_gather(attended, 'mp', axis=1, tiled=True), final_project...  5.31 us
  transfers between devices with their start and end apart: 5, of which 5 were waited for; matrix products, arithmetic and copies ran while one was open for 4% of the time, Pallas kernels for 0%

commit v1 on v0

--- a/solution.py
+++ b/solution.py
@@ -90,7 +90,10 @@
         own_slots // block_rows * nseq * block_rows + shard * block_rows + own_slots % block_rows
     )
     start_best = jnp.full((memory_pair_portion, asker_cluster, owned), -1e30, jnp.float32)
-    piece = lax.all_gather(paired, "seq", axis=1, tiled=True)
+    size = lax.axis_size("seq")
+    parts = jnp.stack([paired for _ in range(size)])
+    parts = lax.all_to_all(parts, "seq", split_axis=0, concat_axis=0)
+    piece = jnp.concatenate(parts, axis=1)
     best = start_best
     count = piece.shape[1]
     key_piece = piece[0].reshape(count, memory_pair_portion, PER_HEAD_DIM)

time: 202 us -> 180 us (0.89)
  waiting for transfers between devices: 125 us -> 98.6 us
  starting transfers between devices: 13.2 us -> 17 us
  local copies, waits for them, and re-layouts: 9.37 us -> 11.8 us
    all_gather x1 -> x0, waiting for transfers between devices: 34 us -> none  [on_device(): piece = lax.all_gather(paired, 'seq', axis=1, tiled=True)]
    all_to_all x0 -> x1, waiting for transfers between devices: none -> 9.57 us  [on_device(): parts = lax.all_to_all(parts, 'seq', split_axis=0, concat_axis=0)]
    all_to_all x0 -> x1, starting transfers between devices: none -> 3.66 us  [on_device(): parts = lax.all_to_all(parts, 'seq', split_axis=0, concat_axis=0)]
    all_gather x1, waiting for transfers between devices: 26 us -> 23.6 us  [on_device(): lax.all_gather(attended, 'mp', axis=1, tiled=True)]
  transfers between devices with their start and end apart: 5 -> 5, of which waited for: 5 -> 5; matrix products, arithmetic and copies ran while one was open for 4% -> 5% of each run, Pallas kernels for 0% -> 0%
where the time goes in v1:
time: 180 us; the launch traced here: 179 us
  waiting for transfers between devices  98.6 us (55%)
  other arithmetic  20 us (11%)
  starting transfers between devices  17 us (9%)
  matrix products  16.2 us (9%)
  between operations  15.6 us (9%)
  local copies, waits for them, and re-layouts  11.8 us (7%)
    all_to_all x1, waiting for transfers between devices, on_device(): lax.all_to_all(outgoing, 'seq', split_axis=1, concat_axis=1, tiled=True)  32.1 us
    all_gather x1, waiting for transfers between devices, on_device(): whole_rows = lax.all_gather(gathered_rows, 'mp', axis=1, tiled=True)  26.6 us
    all_gather x1, waiting for transfers between devices, on_device(): lax.all_gather(attended, 'mp', axis=1, tiled=True)  23.6 us
    all_to_all x1, waiting for transfers between devices, on_device(): parts = lax.all_to_all(parts, 'seq', split_axis=0, concat_axis=0)  9.57 us
    all_to_all x1, starting transfers between devices, on_device(): lax.all_to_all(outgoing, 'seq', split_axis=1, concat_axis=1, tiled=True)  6.64 us
    all_to_all x1, waiting for transfers between devices, on_device(): lax.all_to_all(outgoing_back, 'seq', split_axis=1, concat_axis=1, tiled=T...  6.57 us
    all_to_all x1, starting transfers between devices, on_device(): lax.all_to_all(outgoing_back, 'seq', split_axis=1, concat_axis=1, tiled=T...  6.53 us
    dot_general x1, matrix products, on_device(): jnp.dot(normed, asker_projection, preferred_element_type=jnp.float32)  5.39 us
  transfers between devices with their start and end apart: 5, of which 5 were waited for; matrix products, arithmetic and copies ran while one was open for 5% of the time, Pallas kernels for 0%

profile of v1, /device:TPU:1, one launch (start us, length us, event | category | flops | bytes accessed | tf_op | source)
XLA Modules:
  0.0 179.3 jit_solution(14133165608141298193)
XLA Ops:
  6.5 0.9 reduce_sum.69
  7.5 0.1 copy.35
  7.6 0.1 reduce.3
  7.7 0.6 and_select_fusion.4
  8.3 0.6 iota_compare_fusion.1
  9.0 0.7 compare_select_fusion
  9.7 2.6 %gather_fusion = bf16[256,512]{1,0:T(8,128)(2,1)S(1)} fusion(bf16[1024,512]{1,0:T(8,128)(2,1)} %param.10, s32[1024]{0:T(1024)S(1)} %pad_clamp_fusion.2), kind=kCustom, calls=%fused_computation | custom fusion | bytes 525312 | tf_op jit(solution)/shard_map/gather | solution.py:60
  12.3 0.8 broadcast_select_fusion
  13.1 0.6 fusion.52
  15.6 26.6 %all-gather.3.cloned.1.call-done = bf16[256,4096]{1,0:T(8,128)(2,1)} async-done(((bf16[256,512]{1,0:T(8,128)(2,1)}), bf16[256,4096]{1,0:T(8,128)(2,1)}) %all-gather.3.cloned.1.call-update) | async-done | bytes 2097168 | tf_op jit(solution)/shard_map/all_gather | solution.py:62
  42.3 2.4 %fusion.7 = bf16[2,16,8,4096]{3,2,1,0:T(8,128)(2,1)S(1)} fusion(s32[]{:T(128)S(6)} %select_n.208, bf16[2,16,8,4096]{3,2,1,0:T(8,128)(2,1)} %bitcast.124), kind=kLoop, calls=%fused_computation.15 | loop fusion | flops 1048576 | bytes 4194308 | tf_op jit(solution)/shard_map/jit(_roll_dynamic)/concatenate | solution.py:63
  44.6 1.5 copy.47
  46.1 6.6 %all-to-all-start = ((bf16[2,16,8,4096]{3,2,0,1:T(8,128)(2,1)}), bf16[2,16,8,4096]{3,2,0,1:T(8,128)(2,1)S(1)}, u32[]{:S(2)}, u32[]{:S(2)}) async-start(bf16[2,16,8,4096]{3,2,0,1:T(8,128)(2,1)} %copy.47), calls=%async_computation | async-start | bytes 4194304 | tf_op jit(solution)/shard_map/all_to_all | solution.py:66
  52.8 0.2 convert_reduce_fusion
  53.0 0.2 select_reduce_fusion
  53.2 32.1 %all-to-all-done = bf16[2,16,8,4096]{3,2,0,1:T(8,128)(2,1)S(1)} async-done(((bf16[2,16,8,4096]{3,2,0,1:T(8,128)(2,1)}), bf16[2,16,8,4096]{3,2,0,1:T(8,128)(2,1)S(1)}, u32[]{:S(2)}, u32[]{:S(2)}) %all-to-all-start) | async-done | bytes 2097184 | tf_op jit(solution)/shard_map/all_to_all | solution.py:66
  85.4 1.5 copy.38
  86.9 2.2 %gather_fusion.1 = bf16[16,8,4096]{2,1,0:T(8,128)(2,1)S(1)} fusion(bf16[32,8,4096]{2,1,0:T(8,128)(2,1)} %bitcast.122, s32[1024]{0:T(1024)S(1)} %pad_clamp_fusion.1), kind=kCustom, calls=%fused_computation.1 | custom fusion | bytes 2097216 | tf_op jit(solution)/shard_map/gather | solution.py:22
  89.1 0.3 multiply_reduce_fusion
  89.4 0.1 rsqrt.12
  89.5 0.5 fusion.11
  90.0 0.3 copy-done.5
  90.3 0.5 fusion.12
  90.8 1.2 stack.11
  92.0 3.7 %all-to-all-start.1 = ((bf16[16,2,128,128]{3,2,1,0:T(8,128)(2,1)}), bf16[16,2,128,128]{3,2,1,0:T(8,128)(2,1)S(1)}, u32[]{:S(2)}, u32[]{:S(2)}) async-start(bf16[16,2,128,128]{3,2,1,0:T(8,128)(2,1)} %stack.11), calls=%async_computation.1 | async-start | bytes 2097152 | tf_op jit(solution)/shard_map/all_to_all | solution.py:95
  95.7 0.2 all-gather.5.cloned.1.call-start
  95.9 0.3 broadcast_compare_fusion
  96.3 5.4 %fusion.8 = bf16[16,8,8,128]{3,2,1,0:T(8,128)(2,1)} fusion(bf16[4096,1024]{1,0:T(8,128)(2,1)} %param.13, bf16[16,8,4096]{2,1,0:T(8,128)(2,1)S(1)} %gather_fusion.1, f32[4096]{0:T(1024)S(1)} %convert_element_type.49, f32[128]{0:T(128)S(1)} %rsqrt.12), kind=kOutput, calls=%fused_computation.20 | convolution fusion | flops 1075970048 | bytes 9716224 | tf_op jit(solution)/shard_map/dot_general | solution.py:72
  101.7 9.6 %all-to-all-done.1 = bf16[16,2,128,128]{3,2,1,0:T(8,128)(2,1)S(1)} async-done(((bf16[16,2,128,128]{3,2,1,0:T(8,128)(2,1)}), bf16[16,2,128,128]{3,2,1,0:T(8,128)(2,1)S(1)}, u32[]{:S(2)}, u32[]{:S(2)}) %all-to-all-start.1) | async-done | bytes 1048608 | tf_op jit(solution)/shard_map/all_to_all | solution.py:95
  111.3 0.9 copy-done.2
  112.2 1.3 fusion
  113.5 2.1 %fusion.1 = f32[8,128]{1,0:T(8,128)S(1)} fusion(f32[2048,128,8]{1,0,2:T(8,128)S(1)} %get-tuple-element.12, f32[8,128]{1,0:T(8,128)S(1)} %broadcast_maximum_fusion, f32[8]{0:T(128)S(1)} %broadcast_multiply_fusion, pred[128,2048]{0,1:T(8,128)(4,1)S(1)} %broadcast_compare_fusion), kind=kLoop, calls=%fused_computation.8 | loop fusion | flops 10484736 | bytes 8658976 | tf_op jit(solution)/shard_map/reduce_sum | solution.py:112
  115.6 2.9 %fusion.21 = bf16[8,128,128]{1,2,0:T(8,128)(2,1)} fusion(bf16[2048,128,1]{1,0,2:T(8,128)(2,1)S(1)} %bitcast.127, f32[2048,128,8]{1,0,2:T(8,128)S(1)} %get-tuple-element.12, f32[8,128]{1,0:T(8,128)S(1)} %broadcast_maximum_fusion, f32[8]{0:T(128)S(1)} %broadcast_multiply_fusion, pred[128,2048]{0,1:T(8,128)(4,1)S(1)} %broadcast_compare_fusion, ...), kind=kOutput, calls=%fused_computation.34 | convolution fusion | flops 547618816 | bytes 9445408 | tf_op jit(solution)/shard_map/ngqk,knd->ngqd/dot_general | solution.py:113
  118.6 0.1 compare_select_fusion.1
  118.7 0.1 reshape.608
  118.8 0.4 fusion.16
  119.2 23.6 %all-gather.5.cloned.1.call-done = bf16[128,8192]{0,1:T(8,128)(2,1)} async-done(((bf16[128,1024]{0,1:T(8,128)(2,1)}), bf16[128,8192]{0,1:T(8,128)(2,1)}) %all-gather.5.cloned.1.call-update) | async-done | bytes 2097168 | tf_op jit(solution)/shard_map/all_gather | solution.py:126
  142.8 5.3 %fusion.10 = bf16[16,8,512]{2,1,0:T(8,128)(2,1)S(1)} fusion(bf16[128,8192]{0,1:T(8,128)(2,1)} %all-gather.5.cloned.1.call-done, bf16[8192,512]{1,0:T(8,128)(2,1)} %param.16, f32[128]{0:T(128)S(1)} %fusion.16), kind=kOutput, calls=%fused_computation.22 | convolution fusion | flops 1073872896 | bytes 10617344 | tf_op jit(solution)/shard_map/dot_general | solution.py:125
  148.2 0.6 gather_fusion.2
  148.7 0.1 broadcast_select_fusion.1
  148.8 0.7 copy.42
  149.6 6.5 %all-to-all-start.2 = ((bf16[2,16,8,512]{3,2,0,1:T(8,128)(2,1)}), bf16[2,16,8,512]{3,2,0,1:T(8,128)(2,1)S(1)}, u32[]{:S(2)}, u32[]{:S(2)}) async-start(bf16[2,16,8,512]{3,2,0,1:T(8,128)(2,1)} %copy.42), calls=%async_computation.2 | async-start | bytes 524288 | tf_op jit(solution)/shard_map/all_to_all | solution.py:132
  156.1 1.6 convert_element_type.45
  157.8 6.6 %all-to-all-done.2 = bf16[2,16,8,512]{3,2,0,1:T(8,128)(2,1)S(1)} async-done(((bf16[2,16,8,512]{3,2,0,1:T(8,128)(2,1)}), bf16[2,16,8,512]{3,2,0,1:T(8,128)(2,1)S(1)}, u32[]{:S(2)}, u32[]{:S(2)}) %all-to-all-start.2) | async-done | bytes 262176 | tf_op jit(solution)/shard_map/all_to_all | solution.py:132
  164.4 0.1 fusion.26
  164.5 0.1 bitcast_select_fusion.1
  164.6 5.2 %scatter_custom_fusion = f32[1024,512]{1,0:T(8,128)} fusion(f32[1024,512]{1,0:T(8,128)} %convert_element_type.45, s32[256]{0:T(256)S(1)} %bitcast.130, bf16[256,512]{1,0:T(8,128)(2,1)S(1)} %bitcast_select_fusion.1), kind=kCustom, calls=%fused_computation.37 | custom fusion | flops 262144 | bytes 2359296 | tf_op jit(solution)/shard_map/scatter-add | solution.py:136
  169.8 2.7 %convert_element_type.59 = bf16[1024,512]{1,0:T(8,128)(2,1)} convert(f32[1024,512]{1,0:T(8,128)} %scatter_custom_fusion) | non-fusion elementwise | flops 524288 | bytes 3145728 | tf_op jit(solution)/shard_map/convert_element_type | solution.py:138
  (33 shorter events, 0.4 us)
Async XLA Ops:
  6.5 83.0 %copy-start = (bf16[4096,128]{1,0:T(8,128)(2,1)S(1)}, bf16[4096,128]{1,0:T(8,128)(2,1)}, u32[]{:S(2)}) copy-start(bf16[4096,128]{1,0:T(8,128)(2,1)} %param.14) | copy-start | bytes 3145732
  6.5 35.7 %all-gather.3.cloned.1.call-start = ((), (), s32[]{:S(2)}) async-start(), calls=%async_computation.3 | async-start | bytes 2359296 | tf_op jit(solution)/shard_map/all_gather | solution.py:62
  46.1 6.7 %copy-start.3 = (bf16[4096]{0:T(1024)(128)(2,1)S(1)}, bf16[4096]{0:T(1024)(128)(2,1)}, u32[]{:S(2)}) copy-start(bf16[4096]{0:T(1024)(128)(2,1)} %param.11) | copy-start | bytes 24580
  46.1 7.1 %copy-start.6 = (f32[8]{0:T(128)S(1)}, f32[8]{0:T(128)}, u32[]{:S(2)}) copy-start(f32[8]{0:T(128)} %param.17) | copy-start | bytes 100
  46.1 39.3 %all-to-all-start = ((bf16[2,16,8,4096]{3,2,0,1:T(8,128)(2,1)}), bf16[2,16,8,4096]{3,2,0,1:T(8,128)(2,1)S(1)}, u32[]{:S(2)}, u32[]{:S(2)}) async-start(bf16[2,16,8,4096]{3,2,0,1:T(8,128)(2,1)} %copy.47), calls=%async_computation | async-start | bytes 4194304 | tf_op jit(solution)/shard_map/all_to_all | solution.py:66
  89.1 1.2 copy-start.5
  92.0 19.2 %all-to-all-start.1 = ((bf16[16,2,128,128]{3,2,1,0:T(8,128)(2,1)}), bf16[16,2,128,128]{3,2,1,0:T(8,128)(2,1)S(1)}, u32[]{:S(2)}, u32[]{:S(2)}) async-start(bf16[16,2,128,128]{3,2,1,0:T(8,128)(2,1)} %stack.11), calls=%async_computation.1 | async-start | bytes 2097152 | tf_op jit(solution)/shard_map/all_to_all | solution.py:95
  95.7 47.1 %all-gather.5.cloned.1.call-start = ((), (), s32[]{:S(2)}) async-start(), calls=%async_computation.4 | async-start | bytes 2359296 | tf_op jit(solution)/shard_map/all_gather | solution.py:126
  111.2 1.0 copy-start.2
  115.6 2.9 %copy-start.4 = (bf16[4096]{0:T(1024)(128)(2,1)S(1)}, bf16[4096]{0:T(1024)(128)(2,1)}, u32[]{:S(2)}) copy-start(bf16[4096]{0:T(1024)(128)(2,1)} %param.12) | copy-start | bytes 24580
  148.1 8.0 %copy-start.1 = (bf16[1024,512]{1,0:T(8,128)(2,1)S(1)}, bf16[1024,512]{1,0:T(8,128)(2,1)}, u32[]{:S(2)}) copy-start(bf16[1024,512]{1,0:T(8,128)(2,1)} %param.10) | copy-start | bytes 3145732
  149.6 14.8 %all-to-all-start.2 = ((bf16[2,16,8,512]{3,2,0,1:T(8,128)(2,1)}), bf16[2,16,8,512]{3,2,0,1:T(8,128)(2,1)S(1)}, u32[]{:S(2)}, u32[]{:S(2)}) async-start(bf16[2,16,8,512]{3,2,0,1:T(8,128)(2,1)} %copy.42), calls=%async_computation.2 | async-start | bytes 524288 | tf_op jit(solution)/shard_map/all_to_all | solution.py:132
Sparse Core Ops, SparseCore 0:
  13.2 29.0 all-gather.2
  118.6 24.1 all-gather.4
